TPU v7x, 32 devices: a whole 2x2x4 slice. The times are simulated.
32 devices in a mesh: ctx: 4 (over z), head: 2 (over x), dp: 4 (over y, core).
Axes of the slice: x: 2, y: 2, z: 4, core: 2. Of those that a mesh axis runs over, the one named last changes fastest.
Arguments:
- queries: bfloat16 [2048, 4096], P(('dp', 'ctx'), 'head'), parts along dimension 0, may hold values from -6 to 6
- key_rows: bfloat16 [2048, 4096], P(('dp', 'ctx'), 'head'), parts along dimension 0, may hold values from -6 to 6
- value_rows: bfloat16 [2048, 4096], P(('dp', 'ctx'), 'head'), parts along dimension 0, may hold values from -6 to 6
- gate_values: bfloat16 [2048, 4096], P(('dp', 'ctx'), 'head'), parts along dimension 0, may hold values from -6 to 6
- cotangent: bfloat16 [2048, 4096], P(('dp', 'ctx'), 'head'), parts along dimension 0, may hold values from -6 to 6
- decay_rates: float32 [16, 4096], P(None, 'head'), may hold values from 0 to 1, as said below
- residues: float32 [16, 4096], P(None, 'head'), may hold values from -4 to 4
- skip_gain: float32 [4096], P('head'), may hold values from -6 to 6
Outputs:
- queries_adjoint: bfloat16 [2048, 4096], P(('dp', 'ctx'), 'head'), parts along dimension 0
- keys_adjoint: bfloat16 [2048, 4096], P(('dp', 'ctx'), 'head'), parts along dimension 0
- values_adjoint: bfloat16 [2048, 4096], P(('dp', 'ctx'), 'head'), parts along dimension 0
- gate_adjoint: bfloat16 [2048, 4096], P(('dp', 'ctx'), 'head'), parts along dimension 0
- residues_adjoint: float32 [64, 4096], P('dp', 'head'), parts along dimension 0
There are 4 independent parts, one for each index of `dp`. A program takes and returns all parts, laid end to end along the dimension named above; an argument that names none is the same for every part. Nothing has to cross between parts.
Inputs may be any that keep to these rules, and one draw needn't show every extreme that they name: `decay_rates`: every rate lies between 0.6 / 512 and 1/16 per position.
All inputs are finite; a program needn't handle non-finite values.
Results may differ from a plain program's by a relative error of at most 0.0094.
Values may be sent and summed in bfloat16 or wider, within the bound.
A program may use at most 128 MiB of HBM per device.

v0:
```python
import functools
import math

import jax
import jax.numpy as jnp
from jax import lax
from jax.experimental import pallas as pl
from jax.experimental.pallas import tpu as pltpu
from jax.sharding import PartitionSpec as P

HEAD = 128
WIN = 4
SEGS = 8
POLE_GROUP = 8
MESH = pl.DeviceIdType.MESH


def decay_gap(x):
    inner = 1.0 - x * (1.0 / 7.0)
    for order in (6.0, 5.0, 4.0, 3.0, 2.0):
        inner = 1.0 - x * (1.0 / order) * inner
    return x * inner


def row_of(ref, kind, pole):
    return jnp.broadcast_to(ref[kind, pl.ds(pole, 1), :], (SEGS, HEAD))


def periodic_start(ends, par_ref, pole, backward):
    total = ends
    for power, kind in ((1, 3), (2, 4), (4, 5)):
        shift = SEGS - power if backward else power
        total = total + row_of(par_ref, kind, pole) * pltpu.roll(total, shift, 0)
    total = total * row_of(par_ref, 6, pole)
    return pltpu.roll(total, SEGS - 1 if backward else 1, 0)


def segment_ends(x_ref, par_ref, poles, steps, backward, unroll=4):
    lams = [row_of(par_ref, 0, pole) for pole in range(poles)]

    def body(index, states):
        for sub in range(unroll):
            step = index * unroll + sub
            if backward:
                step = steps - 1 - step
            x = x_ref[pl.ds(step, SEGS, stride=steps), :]
            states = tuple(lam * state + x for lam, state in zip(lams, states))
        return states

    zeros = tuple(jnp.zeros((SEGS, HEAD), jnp.float32) for _ in range(poles))
    ends = lax.fori_loop(0, steps // unroll, body, zeros)
    return [periodic_start(end, par_ref, pole, backward) for pole, end in enumerate(ends)]


def tree_sum(terms):
    terms = list(terms)
    while len(terms) > 1:
        paired = [a + b for a, b in zip(terms[::2], terms[1::2])]
        if len(terms) % 2:
            paired.append(terms[-1])
        terms = paired
    return terms[0]


def fast_kernel(
    members, local_heads,
    q_ref, k_ref, v_ref, gate_ref, cot_ref, decay_ref, residue_ref, skip_ref,
    dq_ref, dk_ref, dv_ref, dgate_ref, dres_ref,
    stage, inbox, outbox, landed, res_box, res_landed,
    par_ref, delta_ref, y_ref, att_ref, da_ref, dk_acc, dv_acc,
    in_send, in_recv, grad_send, grad_recv, mix_send, mix_recv, res_send, res_recv,
):
    me = lax.axis_index("ctx")
    rows = q_ref.shape[0]
    tokens = rows * members
    steps = tokens // SEGS
    poles = decay_ref.shape[0]
    group = local_heads // members
    scale = 1.0 / math.sqrt(HEAD)

    barrier = pltpu.get_barrier_semaphore()
    for off in range(1, members):
        pl.semaphore_signal(
            barrier, inc=1, device_id={"ctx": lax.rem(me + off, members)}, device_id_type=MESH
        )
    stage[0] = (cot_ref[...].astype(jnp.float32) * gate_ref[...].astype(jnp.float32)).astype(
        jnp.bfloat16
    )
    stage[1] = q_ref[...]
    stage[2] = k_ref[...]
    stage[3] = v_ref[...]
    pl.semaphore_wait(barrier, members - 1)

    def lanes(owner, head):
        return pl.ds(pl.multiple_of((owner * group + head) * HEAD, HEAD), HEAD)

    def rows_of(owner):
        return pl.ds(pl.multiple_of(owner * rows, rows), rows)

    def dest(off):
        return lax.rem(me + off, members)

    def source(off):
        return lax.rem(me + members - off, members)

    def remote(src, dst, send, recv, target):
        return pltpu.make_async_remote_copy(
            src_ref=src, dst_ref=dst, send_sem=send, recv_sem=recv,
            device_id={"ctx": target}, device_id_type=MESH,
        )

    def in_copy(head, off):
        return remote(
            stage.at[:, :, lanes(dest(off), head)], inbox.at[head, :, rows_of(me), :],
            in_send.at[head, off - 1], in_recv.at[head, off - 1], dest(off),
        )

    def in_arrival(head, off):
        return remote(
            stage.at[:, :, lanes(dest(off), head)], inbox.at[head, :, rows_of(source(off)), :],
            in_send.at[head, off - 1], in_recv.at[head, off - 1], dest(off),
        )

    def grad_copy(head, off, owner):
        return remote(
            outbox.at[head, pl.ds(0, 3), rows_of(dest(off)), :],
            landed.at[pl.ds(0, 3), :, lanes(owner, head)],
            grad_send.at[head, off - 1], grad_recv.at[head, off - 1], dest(off),
        )

    def mix_copy(head, off, owner):
        return remote(
            outbox.at[head, pl.ds(3, 1), rows_of(dest(off)), :],
            landed.at[pl.ds(3, 1), :, lanes(owner, head)],
            mix_send.at[head, off - 1], mix_recv.at[head, off - 1], dest(off),
        )

    def res_copy(head, off, owner):
        return remote(
            res_box.at[head], res_landed.at[:, lanes(owner, head)],
            res_send.at[head, off - 1], res_recv.at[head, off - 1], dest(off),
        )

    def send_inputs(head, carry):
        for off in range(1, members):
            in_copy(head, off).start()
        return carry

    lax.fori_loop(0, group, send_inputs, 0)

    def one_head(head, carry):
        mine = lanes(me, head)
        damping = decay_ref[:, mine]
        weights = jnp.sqrt(decay_gap(2.0 * damping))
        par_ref[0] = 1.0 - decay_gap(damping)
        par_ref[1] = residue_ref[:, mine] * weights
        par_ref[2] = weights
        par_ref[3] = jnp.exp(-damping * steps)
        par_ref[4] = jnp.exp(-damping * (2 * steps))
        par_ref[5] = jnp.exp(-damping * (4 * steps))
        par_ref[6] = 1.0 / (1.0 - jnp.exp(-damping * tokens))
        skip = jnp.broadcast_to(skip_ref[:, mine], (SEGS, HEAD))
        inbox[head, :, rows_of(me), :] = stage[:, :, mine]
        for off in range(1, members):
            in_arrival(head, off).wait_recv()
        delta_ref[...] = inbox[head, 0].astype(jnp.float32)

        entering = segment_ends(delta_ref, par_ref, poles, steps, True)
        lams = [row_of(par_ref, 0, pole) for pole in range(poles)]
        mixes = [row_of(par_ref, 1, pole) for pole in range(poles)]

        def backward_body(index, states):
            for sub in range(2):
                step = steps - 1 - (index * 2 + sub)
                x = delta_ref[pl.ds(step, SEGS, stride=steps), :]
                states = tuple(lam * state + x for lam, state in zip(lams, states))
                y_ref[pl.ds(step, SEGS, stride=steps), :] = skip * x + tree_sum(
                    mix * state for mix, state in zip(mixes, states)
                )
            return states

        lax.fori_loop(0, steps // 2, backward_body, tuple(entering))
        da_ref[...] = y_ref[...].astype(jnp.bfloat16)

        key_head = inbox[head, 2]
        value_head = inbox[head, 3]
        for block in range(members):
            span = pl.ds(block * rows, rows)
            query = inbox[head, 1, span, :]
            adjoint = da_ref[span, :]
            scores = lax.dot_general(
                query, key_head, (((1,), (1,)), ((), ())), preferred_element_type=jnp.float32
            ) * scale
            raised = jnp.exp(scores - jnp.max(scores, axis=1, keepdims=True))
            probability = raised * (1.0 / jnp.sum(raised, axis=1, keepdims=True))
            rounded = probability.astype(jnp.bfloat16)
            attended = jnp.dot(rounded, value_head, preferred_element_type=jnp.float32)
            att_ref[span, :] = attended.astype(jnp.bfloat16).astype(jnp.float32)
            weight_adjoint = lax.dot_general(
                adjoint, value_head, (((1,), (1,)), ((), ())), preferred_element_type=jnp.float32
            )
            inner = jnp.sum(probability * weight_adjoint, axis=1, keepdims=True)
            score_adjoint = (probability * (weight_adjoint - inner) * scale).astype(jnp.bfloat16)
            outbox[head, 0, span, :] = jnp.dot(
                score_adjoint, key_head, preferred_element_type=jnp.float32
            ).astype(jnp.bfloat16)
            key_part = lax.dot_general(
                score_adjoint, query, (((0,), (0,)), ((), ())), preferred_element_type=jnp.float32
            )
            value_part = lax.dot_general(
                rounded, adjoint, (((0,), (0,)), ((), ())), preferred_element_type=jnp.float32
            )
            if block == 0:
                dk_acc[...] = key_part
                dv_acc[...] = value_part
            else:
                dk_acc[...] += key_part
                dv_acc[...] += value_part
        outbox[head, 1] = dk_acc[...].astype(jnp.bfloat16)
        outbox[head, 2] = dv_acc[...].astype(jnp.bfloat16)
        for off in range(1, members):
            grad_copy(head, off, me).start()

        entering_forward = segment_ends(att_ref, par_ref, poles, steps, False)
        for first in range(0, poles, POLE_GROUP):
            chosen = range(first, first + POLE_GROUP)
            group_lams = [row_of(par_ref, 0, pole) for pole in chosen]
            group_mixes = [row_of(par_ref, 1, pole) for pole in chosen]

            def forward_body(index, item, first=first, lams=group_lams, mixes=group_mixes):
                states, sums = item
                for sub in range(2):
                    step = index * 2 + sub
                    here = pl.ds(step, SEGS, stride=steps)
                    x = att_ref[here, :]
                    delta = delta_ref[here, :]
                    states = tuple(lam * state + x for lam, state in zip(lams, states))
                    sums = tuple(total + delta * state for total, state in zip(sums, states))
                    base = skip * x if first == 0 else y_ref[here, :]
                    y_ref[here, :] = base + tree_sum(
                        mix * state for mix, state in zip(mixes, states)
                    )
                return states, sums

            zeros = tuple(jnp.zeros((SEGS, HEAD), jnp.float32) for _ in chosen)
            starts = tuple(entering_forward[pole] for pole in chosen)
            unused, sums = lax.fori_loop(0, steps // 2, forward_body, (starts, zeros))
            for pole, total in zip(chosen, sums):
                res_box[head, pl.ds(pole, 1), :] = (
                    jnp.sum(total, axis=0, keepdims=True) * par_ref[2, pl.ds(pole, 1), :]
                )
        outbox[head, 3] = y_ref[...].astype(jnp.bfloat16)
        for off in range(1, members):
            mix_copy(head, off, me).start()
            res_copy(head, off, me).start()
        landed[:, :, mine] = outbox[head, :, rows_of(me), :]
        res_landed[:, mine] = res_box[head]
        return carry

    lax.fori_loop(0, group, one_head, 0)

    def finish(head, carry):
        for off in range(1, members):
            grad_copy(head, off, source(off)).wait_recv()
            mix_copy(head, off, source(off)).wait_recv()
            res_copy(head, off, source(off)).wait_recv()
        return carry

    lax.fori_loop(0, group, finish, 0)
    dq_ref[...] = landed[0]
    dk_ref[...] = landed[1]
    dv_ref[...] = landed[2]
    dgate_ref[...] = (
        cot_ref[...].astype(jnp.float32) * landed[3].astype(jnp.float32)
    ).astype(jnp.bfloat16)
    dres_ref[...] = res_landed[...]

    def sent(head, carry):
        for off in range(1, members):
            in_copy(head, off).wait_send()
            grad_copy(head, off, me).wait_send()
            mix_copy(head, off, me).wait_send()
            res_copy(head, off, me).wait_send()
        return carry

    lax.fori_loop(0, group, sent, 0)


def fast_local(queries, key_rows, value_rows, gate_values, cotangent, decay_rates, residues, skip_gain):
    members = lax.axis_size("ctx")
    rows, channels = queries.shape
    local_heads = channels // HEAD
    group = local_heads // members
    tokens = rows * members
    poles = decay_rates.shape[0]
    vmem = pl.BlockSpec(memory_space=pltpu.VMEM)
    wide = jax.ShapeDtypeStruct((rows, channels), jnp.bfloat16)
    sems = pltpu.SemaphoreType.DMA((group, members - 1))
    return pl.pallas_call(
        functools.partial(fast_kernel, members, local_heads),
        out_shape=(wide, wide, wide, wide, jax.ShapeDtypeStruct((poles, channels), jnp.float32)),
        in_specs=[vmem] * 8,
        out_specs=(vmem,) * 5,
        scratch_shapes=[
            pltpu.VMEM((4, rows, channels), jnp.bfloat16),
            pltpu.VMEM((group, 4, tokens, HEAD), jnp.bfloat16),
            pltpu.VMEM((group, 4, tokens, HEAD), jnp.bfloat16),
            pltpu.VMEM((4, rows, channels), jnp.bfloat16),
            pltpu.VMEM((group, poles, HEAD), jnp.float32),
            pltpu.VMEM((poles, channels), jnp.float32),
            pltpu.VMEM((7, poles, HEAD), jnp.float32),
            pltpu.VMEM((tokens, HEAD), jnp.float32),
            pltpu.VMEM((tokens, HEAD), jnp.float32),
            pltpu.VMEM((tokens, HEAD), jnp.float32),
            pltpu.VMEM((tokens, HEAD), jnp.bfloat16),
            pltpu.VMEM((tokens, HEAD), jnp.float32),
            pltpu.VMEM((tokens, HEAD), jnp.float32),
        ] + [sems] * 8,
        compiler_params=pltpu.CompilerParams(
            collective_id=0, has_side_effects=True, vmem_limit_bytes=48 * 1024 * 1024
        ),
    )(queries, key_rows, value_rows, gate_values, cotangent, decay_rates, residues,
      skip_gain.reshape(1, channels))


def passed_along(array, axis, by):
    length = lax.axis_size(axis)
    return lax.ppermute(array, axis, [(i, (i + by) % length) for i in range(length)])


def window_mask(row_count):
    row_ids = jnp.arange(row_count)[:, None, None]
    lag_ids = jnp.arange(WIN + 1)[None, :, None]
    column_ids = jnp.arange(row_count)[None, None, :]
    return ((lag_ids > 0) | (column_ids <= row_ids)) & ((lag_ids < WIN) | (column_ids > row_ids))


def local(queries, key_rows, value_rows, gate_values, cotangent, decay_rates, residues, skip_gain):
    members = lax.axis_size("ctx")
    tok_rows, channels = queries.shape
    local_heads = channels // HEAD
    scale_factor = 1.0 / math.sqrt(HEAD)
    weights = jnp.sqrt(-jnp.expm1(-2.0 * decay_rates))
    mixing = residues * weights
    loop_gap = -jnp.expm1(-decay_rates * (tok_rows * members))
    device_decay = jnp.exp(-decay_rates * tok_rows)
    piece_rows = min(128, tok_rows)
    pieces = tok_rows // piece_rows
    offsets = jnp.arange(piece_rows, dtype=jnp.float32)[:, None, None]
    piece_index = jnp.arange(pieces, dtype=jnp.float32)[:, None, None]
    start_weights = jnp.exp(-decay_rates[None] * offsets)
    growth = jnp.exp(decay_rates[None] * offsets)
    delta_rows = cotangent.astype(jnp.float32) * gate_values.astype(jnp.float32)
    blocks_delta = delta_rows.reshape(pieces, piece_rows, channels)
    piece_starts = jnp.einsum(
        "qpc,mqc->mpc", start_weights, blocks_delta, precision=lax.Precision.HIGHEST
    )
    head_state = jnp.sum(
        jnp.exp(-decay_rates[None] * (piece_index * piece_rows)) * piece_starts, axis=0
    )

    def backward_turn(turn_index, moving):
        return passed_along(device_decay * moving + head_state, "ctx", -1)

    incoming = lax.fori_loop(0, members, backward_turn, jnp.zeros_like(head_state)) / loop_gap

    def backward_step(carried, segment):
        local_part = growth * lax.cumsum(start_weights * segment[:, None, :], axis=0, reverse=True)
        states = local_part + jnp.exp(-decay_rates[None] * (piece_rows - offsets)) * carried[None]
        mixture = jnp.sum(mixing[None] * states, axis=1) + skip_gain[None] * segment
        return (states[0], mixture)

    unused_state, adjoint_rows = lax.scan(backward_step, incoming, blocks_delta, reverse=True)
    attended_adjoint = adjoint_rows.reshape(tok_rows, channels).astype(jnp.bfloat16)
    key_value = jnp.stack([key_rows, value_rows])
    window = [key_value]
    moving = key_value
    for lag_index in range(WIN):
        moving = passed_along(moving, "ctx", 1)
        window.append(moving)
    stacked = jnp.stack(window)
    key_window = stacked[:, 0]
    value_window = stacked[:, 1]
    allowed = window_mask(tok_rows)
    attended_parts = []
    query_adjoints = []
    key_partials = []
    value_partials = []
    for head_index in range(local_heads):
        first = head_index * HEAD
        query_head = queries[:, first : first + HEAD]
        key_head = key_window[:, :, first : first + HEAD]
        value_head = value_window[:, :, first : first + HEAD]
        adjoint_head = attended_adjoint[:, first : first + HEAD]
        scores = (
            jnp.einsum("re,kse->rks", query_head, key_head, preferred_element_type=jnp.float32)
            * scale_factor
        )
        masked = jnp.where(allowed, scores, -jnp.inf)
        row_top = jnp.max(masked, axis=(1, 2), keepdims=True)
        raised = jnp.exp(masked - row_top)
        probability = raised / jnp.sum(raised, axis=(1, 2), keepdims=True)
        rounded_prob = probability.astype(jnp.bfloat16)
        attended_parts.append(
            jnp.einsum(
                "rks,kse->re", rounded_prob, value_head, preferred_element_type=jnp.float32
            ).astype(jnp.bfloat16)
        )
        weight_adjoint = jnp.einsum(
            "re,kse->rks", adjoint_head, value_head, preferred_element_type=jnp.float32
        )
        inner_sum = jnp.sum(probability * weight_adjoint, axis=(1, 2), keepdims=True)
        score_adjoint = (probability * (weight_adjoint - inner_sum) * scale_factor).astype(
            jnp.bfloat16
        )
        query_adjoints.append(
            jnp.einsum(
                "rks,kse->re", score_adjoint, key_head, preferred_element_type=jnp.float32
            ).astype(jnp.bfloat16)
        )
        key_partials.append(
            jnp.einsum(
                "rks,re->kse", score_adjoint, query_head, preferred_element_type=jnp.float32
            ).astype(jnp.bfloat16)
        )
        value_partials.append(
            jnp.einsum(
                "rks,re->kse", rounded_prob, adjoint_head, preferred_element_type=jnp.float32
            ).astype(jnp.bfloat16)
        )
    attended = jnp.concatenate(attended_parts, axis=1)
    queries_adjoint = jnp.concatenate(query_adjoints, axis=1)
    partials = jnp.stack(
        [jnp.concatenate(key_partials, axis=2), jnp.concatenate(value_partials, axis=2)], axis=1
    )
    collected = partials[0].astype(jnp.float32)
    for lag_index in range(1, WIN + 1):
        collected = collected + passed_along(partials[lag_index], "ctx", -lag_index).astype(
            jnp.float32
        )
    keys_adjoint = collected[0].astype(jnp.bfloat16)
    values_adjoint = collected[1].astype(jnp.bfloat16)
    signal = attended.astype(jnp.float32)
    blocks_signal = signal.reshape(pieces, piece_rows, channels)
    end_weights = jnp.exp(-decay_rates[None] * (piece_rows - 1.0 - offsets))
    piece_ends = jnp.einsum(
        "qpc,mqc->mpc", end_weights, blocks_signal, precision=lax.Precision.HIGHEST
    )
    tail_state = jnp.sum(
        jnp.exp(-decay_rates[None] * ((pieces - 1.0 - piece_index) * piece_rows)) * piece_ends,
        axis=0,
    )

    def forward_turn(turn_index, moving):
        return passed_along(device_decay * moving + tail_state, "ctx", 1)

    arriving = lax.fori_loop(0, members, forward_turn, jnp.zeros_like(tail_state)) / loop_gap
    entering = jnp.exp(-decay_rates[None] * (offsets + 1.0))

    def forward_step(carried, step_item):
        segment, matched = step_item
        local_part = start_weights * jnp.cumsum(growth * segment[:, None, :], axis=0)
        states = local_part + entering * carried[None]
        mixture = jnp.sum(mixing[None] * states, axis=1) + skip_gain[None] * segment
        product = jnp.sum(weights[None] * matched[:, None, :] * states, axis=0)
        return (states[-1], (mixture, product))

    closing, (mixed_rows, products) = lax.scan(
        forward_step, arriving, (blocks_signal, blocks_delta)
    )
    gate_adjoint = (cotangent.astype(jnp.float32) * mixed_rows.reshape(tok_rows, channels)).astype(
        jnp.bfloat16
    )
    residues_adjoint = lax.psum(jnp.sum(products, axis=0), "ctx")
    return (queries_adjoint, keys_adjoint, values_adjoint, gate_adjoint, residues_adjoint)


def solution(mesh):
    in_specs = (
        P(("dp", "ctx"), "head"),
        P(("dp", "ctx"), "head"),
        P(("dp", "ctx"), "head"),
        P(("dp", "ctx"), "head"),
        P(("dp", "ctx"), "head"),
        P(None, "head"),
        P(None, "head"),
        P("head"),
    )
    out_specs = (
        P(("dp", "ctx"), "head"),
        P(("dp", "ctx"), "head"),
        P(("dp", "ctx"), "head"),
        P(("dp", "ctx"), "head"),
        P("dp", "head"),
    )
    members = mesh.shape["ctx"]

    def chosen(*arrays):
        rows, channels = arrays[0].shape
        whole = members == WIN and rows % 128 == 0 and (channels // HEAD) % members == 0
        return (fast_local if whole and arrays[5].shape[0] % POLE_GROUP == 0 else local)(*arrays)

    return jax.shard_map(chosen, mesh=mesh, in_specs=in_specs, out_specs=out_specs, check_vma=False)
```

profile of v0, /device:TPU:0, one launch (start us, length us, event | category | flops | bytes accessed | tf_op | source)
XLA Modules:
  0.0 111.3 jit_solution(6586652334169488153)
XLA Ops:
  0.6 0.0 copy-start
  0.6 1.0 copy-done
  1.7 0.0 copy-start.1
  1.7 1.0 copy-done.1
  2.7 0.0 copy-start.2
  2.7 1.0 copy-done.2
  3.8 0.0 copy-start.3
  3.8 1.0 copy-done.3
  4.8 0.0 copy-start.4
  4.8 1.0 copy-done.4
  5.8 0.0 copy-start.5
  5.8 0.9 copy-done.5
  6.8 0.0 copy-start.6
  6.8 0.9 copy-done.6
  7.7 0.0 copy-start.7
  7.7 0.7 copy-done.7
  8.4 99.1 %shard_map.119 = (bf16[128,2048]{1,0:T(8,128)(2,1)S(1)}, bf16[128,2048]{1,0:T(8,128)(2,1)S(1)}, bf16[128,2048]{1,0:T(8,128)(2,1)S(1)}, bf16[128,2048]{1,0:T(8,128)(2,1)S(1)}, f32[16,2048]{1,0:T(8,128)S(1)}) custom-call(bf16[128,2048]{1,0:T(8,128)(2,1)S(1)} %copy-done, bf16[128,2048]{1,0:T(8,128)(2,1)S(1)} %copy-done.1, bf16[128,2048]{1,0:T(8,128)(2,1)S(1)} %copy-done.2, ...), custom_call_target="tpu_custom_call" | custom-call | tf_op jit(solution)/shard_map/pallas_call | solution.py:299
  107.5 0.8 copy.18
  108.3 0.8 copy.19
  109.1 0.8 copy.20
  109.9 0.8 copy.21
  110.7 0.7 copy.22
Async XLA Ops:
  0.6 1.0 copy-start
  1.7 1.0 copy-start.1
  2.7 1.0 copy-start.2
  3.8 1.0 copy-start.3
  4.8 1.0 copy-start.4
  5.8 0.9 copy-start.5
  6.8 0.9 copy-start.6
  7.7 0.7 copy-start.7
where the time goes:
time: 112 us; the launch traced here: 111 us
  Pallas kernels  99.1 us (88%)
  local copies, waits for them, and re-layouts  11.5 us (10%)
    pallas_call x1, Pallas kernels, fast_local(): pl.pallas_call(functools.partial(fast_kernel, members, local_heads), out_...  99.1 us
    unnamed x21, local copies, waits for them, and re-layouts  11.5 us

commit v1 on v0

--- a/solution.py
+++ b/solution.py
@@ -66,33 +66,57 @@
     members, local_heads,
     q_ref, k_ref, v_ref, gate_ref, cot_ref, decay_ref, residue_ref, skip_ref,
     dq_ref, dk_ref, dv_ref, dgate_ref, dres_ref,
-    stage, inbox, outbox, landed, res_box, res_landed,
-    par_ref, delta_ref, y_ref, att_ref, da_ref, dk_acc, dv_acc,
+    stage, inbox, outbox, landed, res_box, res_landed, res_wide,
+    cot_v, gate_v, decay_v, residue_v, skip_v, par_ref, delta_ref, y_ref, att_ref, da_ref, dk_acc, dv_acc,
     in_send, in_recv, grad_send, grad_recv, mix_send, mix_recv, res_send, res_recv,
+    load_sem, stage_sem, out_sem,
 ):
     me = lax.axis_index("ctx")
     rows = q_ref.shape[0]
     tokens = rows * members
     steps = tokens // SEGS
-    poles = decay_ref.shape[0]
+    poles = decay_v.shape[0]
     group = local_heads // members
     scale = 1.0 / math.sqrt(HEAD)
 
+    owned = pl.ds(pl.multiple_of(me * (group * HEAD), HEAD), group * HEAD)
+    loads = [
+        pltpu.make_async_copy(src, dst, load_sem.at[index])
+        for index, (src, dst) in enumerate((
+            (cot_ref, cot_v), (gate_ref, gate_v), (decay_ref.at[:, owned], decay_v),
+            (residue_ref.at[:, owned], residue_v), (skip_ref.at[:, owned], skip_v),
+        ))
+    ]
+    for load in loads[:2]:
+        load.start()
+
+    def lanes(owner, head):
+        return pl.ds(pl.multiple_of((owner * group + head) * HEAD, HEAD), HEAD)
+
+    def stage_copy(head, owner, kind):
+        return pltpu.make_async_copy(
+            (q_ref, k_ref, v_ref)[kind].at[:, lanes(owner, head)],
+            stage.at[head, owner, kind + 1], stage_sem.at[head, owner, kind],
+        )
+
+    def start_stage(head, carry):
+        for owner in range(members):
+            for kind in range(3):
+                stage_copy(head, owner, kind).start()
+        return carry
+
+    start_stage(0, 0)
     barrier = pltpu.get_barrier_semaphore()
     for off in range(1, members):
         pl.semaphore_signal(
             barrier, inc=1, device_id={"ctx": lax.rem(me + off, members)}, device_id_type=MESH
         )
-    stage[0] = (cot_ref[...].astype(jnp.float32) * gate_ref[...].astype(jnp.float32)).astype(
-        jnp.bfloat16
-    )
-    stage[1] = q_ref[...]
-    stage[2] = k_ref[...]
-    stage[3] = v_ref[...]
+    lax.fori_loop(1, group, start_stage, 0)
+    for load in loads[2:]:
+        load.start()
+    for load in loads[:2]:
+        load.wait()
     pl.semaphore_wait(barrier, members - 1)
-
-    def lanes(owner, head):
-        return pl.ds(pl.multiple_of((owner * group + head) * HEAD, HEAD), HEAD)
 
     def rows_of(owner):
         return pl.ds(pl.multiple_of(owner * rows, rows), rows)
@@ -111,56 +135,68 @@
 
     def in_copy(head, off):
         return remote(
-            stage.at[:, :, lanes(dest(off), head)], inbox.at[head, :, rows_of(me), :],
+            stage.at[head, dest(off)], inbox.at[head, :, rows_of(me), :],
             in_send.at[head, off - 1], in_recv.at[head, off - 1], dest(off),
         )
 
     def in_arrival(head, off):
         return remote(
-            stage.at[:, :, lanes(dest(off), head)], inbox.at[head, :, rows_of(source(off)), :],
+            stage.at[head, dest(off)], inbox.at[head, :, rows_of(source(off)), :],
             in_send.at[head, off - 1], in_recv.at[head, off - 1], dest(off),
         )
 
     def grad_copy(head, off, owner):
         return remote(
             outbox.at[head, pl.ds(0, 3), rows_of(dest(off)), :],
-            landed.at[pl.ds(0, 3), :, lanes(owner, head)],
+            landed.at[head, owner, pl.ds(0, 3)],
             grad_send.at[head, off - 1], grad_recv.at[head, off - 1], dest(off),
         )
 
     def mix_copy(head, off, owner):
         return remote(
             outbox.at[head, pl.ds(3, 1), rows_of(dest(off)), :],
-            landed.at[pl.ds(3, 1), :, lanes(owner, head)],
+            landed.at[head, owner, pl.ds(3, 1)],
             mix_send.at[head, off - 1], mix_recv.at[head, off - 1], dest(off),
         )
 
     def res_copy(head, off, owner):
         return remote(
-            res_box.at[head], res_landed.at[:, lanes(owner, head)],
+            res_box.at[head], res_landed.at[head, owner],
             res_send.at[head, off - 1], res_recv.at[head, off - 1], dest(off),
         )
 
+    odd = lax.rem(me, 2)
+    far_first = (2, 3 - 2 * odd, 1 + 2 * odd) if members == 4 else tuple(range(1, members))
+
     def send_inputs(head, carry):
-        for off in range(1, members):
+        for owner in range(members):
+            here = lanes(owner, head)
+            stage[head, owner, 0] = (
+                cot_v[:, here].astype(jnp.float32) * gate_v[:, here].astype(jnp.float32)
+            ).astype(jnp.bfloat16)
+            for kind in range(3):
+                stage_copy(head, owner, kind).wait()
+        for off in far_first:
             in_copy(head, off).start()
         return carry
 
     lax.fori_loop(0, group, send_inputs, 0)
+    for load in loads[2:]:
+        load.wait()
 
     def one_head(head, carry):
-        mine = lanes(me, head)
-        damping = decay_ref[:, mine]
+        mine = pl.ds(pl.multiple_of(head * HEAD, HEAD), HEAD)
+        damping = decay_v[:, mine]
         weights = jnp.sqrt(decay_gap(2.0 * damping))
         par_ref[0] = 1.0 - decay_gap(damping)
-        par_ref[1] = residue_ref[:, mine] * weights
+        par_ref[1] = residue_v[:, mine] * weights
         par_ref[2] = weights
         par_ref[3] = jnp.exp(-damping * steps)
         par_ref[4] = jnp.exp(-damping * (2 * steps))
         par_ref[5] = jnp.exp(-damping * (4 * steps))
         par_ref[6] = 1.0 / (1.0 - jnp.exp(-damping * tokens))
-        skip = jnp.broadcast_to(skip_ref[:, mine], (SEGS, HEAD))
-        inbox[head, :, rows_of(me), :] = stage[:, :, mine]
+        skip = jnp.broadcast_to(skip_v[:, mine], (SEGS, HEAD))
+        inbox[head, :, rows_of(me), :] = stage[head, me]
         for off in range(1, members):
             in_arrival(head, off).wait_recv()
         delta_ref[...] = inbox[head, 0].astype(jnp.float32)
@@ -218,7 +254,7 @@
                 dv_acc[...] += value_part
         outbox[head, 1] = dk_acc[...].astype(jnp.bfloat16)
         outbox[head, 2] = dv_acc[...].astype(jnp.bfloat16)
-        for off in range(1, members):
+        for off in far_first:
             grad_copy(head, off, me).start()
 
         entering_forward = segment_ends(att_ref, par_ref, poles, steps, False)
@@ -246,44 +282,71 @@
             starts = tuple(entering_forward[pole] for pole in chosen)
             unused, sums = lax.fori_loop(0, steps // 2, forward_body, (starts, zeros))
             for pole, total in zip(chosen, sums):
-                res_box[head, pl.ds(pole, 1), :] = (
+                par_ref[7, pl.ds(pole, 1), :] = (
                     jnp.sum(total, axis=0, keepdims=True) * par_ref[2, pl.ds(pole, 1), :]
                 )
+        res_box[head] = par_ref[7].astype(jnp.bfloat16)
         outbox[head, 3] = y_ref[...].astype(jnp.bfloat16)
-        for off in range(1, members):
+        for off in far_first:
             mix_copy(head, off, me).start()
             res_copy(head, off, me).start()
-        landed[:, :, mine] = outbox[head, :, rows_of(me), :]
-        res_landed[:, mine] = res_box[head]
+        landed[head, me] = outbox[head, :, rows_of(me), :]
+        res_landed[head, me] = res_box[head]
         return carry
 
     lax.fori_loop(0, group, one_head, 0)
+
+    def out_copy(head, owner, kind):
+        src = res_wide.at[head, owner] if kind == 4 else landed.at[head, owner, kind]
+        target = (dq_ref, dk_ref, dv_ref, dgate_ref, dres_ref)[kind]
+        return pltpu.make_async_copy(
+            src, target.at[:, lanes(owner, head)], out_sem.at[head, owner, kind]
+        )
 
     def finish(head, carry):
         for off in range(1, members):
             grad_copy(head, off, source(off)).wait_recv()
             mix_copy(head, off, source(off)).wait_recv()
             res_copy(head, off, source(off)).wait_recv()
+        for owner in range(members):
+            landed[head, owner, 3] = (
+                cot_v[:, lanes(owner, head)].astype(jnp.float32)
+                * landed[head, owner, 3].astype(jnp.float32)
+            ).astype(jnp.bfloat16)
+            res_wide[head, owner] = res_landed[head, owner].astype(jnp.float32)
+            for kind in range(5):
+                out_copy(head, owner, kind).start()
         return carry
 
     lax.fori_loop(0, group, finish, 0)
-    dq_ref[...] = landed[0]
-    dk_ref[...] = landed[1]
-    dv_ref[...] = landed[2]
-    dgate_ref[...] = (
-        cot_ref[...].astype(jnp.float32) * landed[3].astype(jnp.float32)
-    ).astype(jnp.bfloat16)
-    dres_ref[...] = res_landed[...]
-
     def sent(head, carry):
         for off in range(1, members):
             in_copy(head, off).wait_send()
             grad_copy(head, off, me).wait_send()
             mix_copy(head, off, me).wait_send()
             res_copy(head, off, me).wait_send()
+        for owner in range(members):
+            for kind in range(5):
+                out_copy(head, owner, kind).wait()
         return carry
 
     lax.fori_loop(0, group, sent, 0)
+
+
+def write_kernel(*refs):
+    sources, targets, sem = refs[:5], refs[5:10], refs[10]
+    copies = []
+    for src, dst in zip(sources, targets):
+        width = src.shape[1] // 2
+        for half in range(2):
+            part = pl.ds(half * width, width)
+            copies.append(
+                pltpu.make_async_copy(src.at[:, part], dst.at[:, part], sem.at[len(copies)])
+            )
+    for copy in copies:
+        copy.start()
+    for copy in copies:
+        copy.wait()
 
 
 def fast_local(queries, key_rows, value_rows, gate_values, cotangent, decay_rates, residues, skip_gain):
@@ -293,34 +356,52 @@
     group = local_heads // members
     tokens = rows * members
     poles = decay_rates.shape[0]
-    vmem = pl.BlockSpec(memory_space=pltpu.VMEM)
     wide = jax.ShapeDtypeStruct((rows, channels), jnp.bfloat16)
     sems = pltpu.SemaphoreType.DMA((group, members - 1))
-    return pl.pallas_call(
+    hbm = pl.BlockSpec(memory_space=pltpu.HBM)
+    shapes = (wide, wide, wide, wide, jax.ShapeDtypeStruct((poles, channels), jnp.float32))
+    results = pl.pallas_call(
         functools.partial(fast_kernel, members, local_heads),
-        out_shape=(wide, wide, wide, wide, jax.ShapeDtypeStruct((poles, channels), jnp.float32)),
-        in_specs=[vmem] * 8,
-        out_specs=(vmem,) * 5,
+        out_shape=shapes,
+        in_specs=[hbm] * 8,
+        out_specs=(hbm,) * 5,
         scratch_shapes=[
-            pltpu.VMEM((4, rows, channels), jnp.bfloat16),
+            pltpu.VMEM((group, members, 4, rows, HEAD), jnp.bfloat16),
             pltpu.VMEM((group, 4, tokens, HEAD), jnp.bfloat16),
             pltpu.VMEM((group, 4, tokens, HEAD), jnp.bfloat16),
-            pltpu.VMEM((4, rows, channels), jnp.bfloat16),
-            pltpu.VMEM((group, poles, HEAD), jnp.float32),
-            pltpu.VMEM((poles, channels), jnp.float32),
-            pltpu.VMEM((7, poles, HEAD), jnp.float32),
+            pltpu.VMEM((group, members, 4, rows, HEAD), jnp.bfloat16),
+            pltpu.VMEM((group, poles, HEAD), jnp.bfloat16),
+            pltpu.VMEM((group, members, poles, HEAD), jnp.bfloat16),
+            pltpu.VMEM((group, members, poles, HEAD), jnp.float32),
+            pltpu.VMEM((rows, channels), jnp.bfloat16),
+            pltpu.VMEM((rows, channels), jnp.bfloat16),
+            pltpu.VMEM((poles, group * HEAD), jnp.float32),
+            pltpu.VMEM((poles, group * HEAD), jnp.float32),
+            pltpu.VMEM((1, group * HEAD), jnp.float32),
+            pltpu.VMEM((8, poles, HEAD), jnp.float32),
             pltpu.VMEM((tokens, HEAD), jnp.float32),
             pltpu.VMEM((tokens, HEAD), jnp.float32),
             pltpu.VMEM((tokens, HEAD), jnp.float32),
             pltpu.VMEM((tokens, HEAD), jnp.bfloat16),
             pltpu.VMEM((tokens, HEAD), jnp.float32),
             pltpu.VMEM((tokens, HEAD), jnp.float32),
-        ] + [sems] * 8,
+        ] + [sems] * 8 + [
+            pltpu.SemaphoreType.DMA((5,)), pltpu.SemaphoreType.DMA((group, members, 3)),
+            pltpu.SemaphoreType.DMA((group, members, 5)),
+        ],
         compiler_params=pltpu.CompilerParams(
-            collective_id=0, has_side_effects=True, vmem_limit_bytes=48 * 1024 * 1024
+            collective_id=0, has_side_effects=True, vmem_limit_bytes=60 * 1024 * 1024
         ),
     )(queries, key_rows, value_rows, gate_values, cotangent, decay_rates, residues,
       skip_gain.reshape(1, channels))
+    return pl.pallas_call(
+        write_kernel,
+        out_shape=shapes,
+        in_specs=[hbm] * 5,
+        out_specs=(hbm,) * 5,
+        scratch_shapes=[pltpu.SemaphoreType.DMA((10,))],
+        compiler_params=pltpu.CompilerParams(vmem_limit_bytes=60 * 1024 * 1024),
+    )(*results)
 
 
 def passed_along(array, axis, by):

time: 112 us -> 170 us (1.52)
  Pallas kernels: 99.1 us -> 169 us
  local copies, waits for them, and re-layouts: 11.5 us -> 0 us
    pallas_call x0 -> x1, Pallas kernels: none -> 68.7 us  [fast_local(): pl.pallas_call(write_kernel, out_shape=shapes, in_specs=[hbm] * 5, out_sp...]
    unnamed x21 -> x0, local copies, waits for them, and re-layouts: 11.5 us -> none
where the time goes in v1:
time: 170 us
  Pallas kernels  169 us (99%)
    pallas_call x1, Pallas kernels, fast_local(): pl.pallas_call(functools.partial(fast_kernel, members, local_heads), out_...  100 us
    pallas_call x1, Pallas kernels, fast_local(): pl.pallas_call(write_kernel, out_shape=shapes, in_specs=[hbm] * 5, out_sp...  68.7 us

profile of v1, /device:TPU:0, one launch (start us, length us, event | category | flops | bytes accessed | tf_op | source)
XLA Modules:
  0.0 169.6 jit_solution(15490934040707813607)
XLA Ops:
  0.6 100.2 %shard_map.119 = (bf16[128,2048]{1,0:T(8,128)(2,1)}, bf16[128,2048]{1,0:T(8,128)(2,1)}, bf16[128,2048]{1,0:T(8,128)(2,1)}, bf16[128,2048]{1,0:T(8,128)(2,1)}, f32[16,2048]{1,0:T(8,128)}) custom-call(bf16[128,2048]{1,0:T(8,128)(2,1)} %q_ref.1, bf16[128,2048]{1,0:T(8,128)(2,1)} %k_ref.1, bf16[128,2048]{1,0:T(8,128)(2,1)} %v_ref.1, bf16[128,2048]{1,0:T(8,128)(2,1)} %gate_ref.1, ...), custom_call_target="tpu_custom_call" | custom-call | tf_op jit(solution)/shard_map/pallas_call | solution.py:363
  100.9 68.7 %shard_map.120 = (bf16[128,2048]{1,0:T(8,128)(2,1)}, bf16[128,2048]{1,0:T(8,128)(2,1)}, bf16[128,2048]{1,0:T(8,128)(2,1)}, bf16[128,2048]{1,0:T(8,128)(2,1)}, f32[16,2048]{1,0:T(8,128)}) custom-call(bf16[128,2048]{1,0:T(8,128)(2,1)} %get-tuple-element.10.refs_0_, bf16[128,2048]{1,0:T(8,128)(2,1)} %get-tuple-element.11.refs_1_, ...), custom_call_target="tpu_custom_call" | custom-call | tf_op jit(solution)/shard_map/pallas_call | solution.py:397

commit v2 on v1

--- a/solution.py
+++ b/solution.py
@@ -12,6 +12,7 @@
 WIN = 4
 SEGS = 8
 POLE_GROUP = 8
+AHEAD = 2
 MESH = pl.DeviceIdType.MESH
 
 
@@ -180,7 +181,7 @@
             in_copy(head, off).start()
         return carry
 
-    lax.fori_loop(0, group, send_inputs, 0)
+    lax.fori_loop(0, min(AHEAD, group), send_inputs, 0)
     for load in loads[2:]:
         load.wait()
 
@@ -199,6 +200,11 @@
         inbox[head, :, rows_of(me), :] = stage[head, me]
         for off in range(1, members):
             in_arrival(head, off).wait_recv()
+
+        @pl.when(head + AHEAD < group)
+        def _():
+            send_inputs(head + AHEAD, 0)
+
         delta_ref[...] = inbox[head, 0].astype(jnp.float32)
 
         entering = segment_ends(delta_ref, par_ref, poles, steps, True)
@@ -334,19 +340,26 @@
 
 
 def write_kernel(*refs):
-    sources, targets, sem = refs[:5], refs[5:10], refs[10]
-    copies = []
-    for src, dst in zip(sources, targets):
+    sources, targets, held, in_sem, out_sem = refs[:5], refs[5:10], refs[10:15], refs[15], refs[16]
+    loads, stores = [], []
+    for src, dst, middle in zip(sources, targets, held):
         width = src.shape[1] // 2
         for half in range(2):
             part = pl.ds(half * width, width)
-            copies.append(
-                pltpu.make_async_copy(src.at[:, part], dst.at[:, part], sem.at[len(copies)])
+            index = len(loads)
+            loads.append(
+                pltpu.make_async_copy(src.at[:, part], middle.at[:, part], in_sem.at[index])
             )
-    for copy in copies:
-        copy.start()
-    for copy in copies:
-        copy.wait()
+            stores.append(
+                pltpu.make_async_copy(middle.at[:, part], dst.at[:, part], out_sem.at[index])
+            )
+    for load in loads:
+        load.start()
+    for load, store in zip(loads, stores):
+        load.wait()
+        store.start()
+    for store in stores:
+        store.wait()
 
 
 def fast_local(queries, key_rows, value_rows, gate_values, cotangent, decay_rates, residues, skip_gain):
@@ -399,7 +412,8 @@
         out_shape=shapes,
         in_specs=[hbm] * 5,
         out_specs=(hbm,) * 5,
-        scratch_shapes=[pltpu.SemaphoreType.DMA((10,))],
+        scratch_shapes=[pltpu.VMEM(shape.shape, shape.dtype) for shape in shapes]
+        + [pltpu.SemaphoreType.DMA((10,))] * 2,
         compiler_params=pltpu.CompilerParams(vmem_limit_bytes=60 * 1024 * 1024),
     )(*results)
 

time: 170 us -> 104 us (0.61)
  Pallas kernels: 169 us -> 103 us
    pallas_call x1, Pallas kernels: 68.7 us -> 2.47 us  [fast_local(): pl.pallas_call(write_kernel, out_shape=shapes, in_specs=[hbm] * 5, out_sp...]
where the time goes in v2:
time: 104 us; the launch traced here: 103 us
  Pallas kernels  103 us (99%)
    pallas_call x1, Pallas kernels, fast_local(): pl.pallas_call(functools.partial(fast_kernel, members, local_heads), out_...  100 us
    pallas_call x1, Pallas kernels, fast_local(): pl.pallas_call(write_kernel, out_shape=shapes, in_specs=[hbm] * 5, out_sp...  2.47 us

profile of v2, /device:TPU:0, one launch (start us, length us, event | category | flops | bytes accessed | tf_op | source)
XLA Modules:
  0.0 103.3 jit_solution(12573670942556306229)
XLA Ops:
  0.6 100.2 %shard_map.119 = (bf16[128,2048]{1,0:T(8,128)(2,1)}, bf16[128,2048]{1,0:T(8,128)(2,1)}, bf16[128,2048]{1,0:T(8,128)(2,1)}, bf16[128,2048]{1,0:T(8,128)(2,1)}, f32[16,2048]{1,0:T(8,128)}) custom-call(bf16[128,2048]{1,0:T(8,128)(2,1)} %q_ref.1, bf16[128,2048]{1,0:T(8,128)(2,1)} %k_ref.1, bf16[128,2048]{1,0:T(8,128)(2,1)} %v_ref.1, bf16[128,2048]{1,0:T(8,128)(2,1)} %gate_ref.1, ...), custom_call_target="tpu_custom_call" | custom-call | tf_op jit(solution)/shard_map/pallas_call | solution.py:376
  100.9 2.5 %shard_map.120 = (bf16[128,2048]{1,0:T(8,128)(2,1)}, bf16[128,2048]{1,0:T(8,128)(2,1)}, bf16[128,2048]{1,0:T(8,128)(2,1)}, bf16[128,2048]{1,0:T(8,128)(2,1)}, f32[16,2048]{1,0:T(8,128)}) custom-call(bf16[128,2048]{1,0:T(8,128)(2,1)} %get-tuple-element.10.refs_0_, bf16[128,2048]{1,0:T(8,128)(2,1)} %get-tuple-element.11.refs_1_, ...), custom_call_target="tpu_custom_call" | custom-call | tf_op jit(solution)/shard_map/pallas_call | solution.py:410

commit v3 on v2

--- a/solution.py
+++ b/solution.py
@@ -44,7 +44,7 @@
             step = index * unroll + sub
             if backward:
                 step = steps - 1 - step
-            x = x_ref[pl.ds(step, SEGS, stride=steps), :]
+            x = x_ref[pl.ds(step, SEGS, stride=steps + 1), :]
             states = tuple(lam * state + x for lam, state in zip(lams, states))
         return states
 
@@ -80,6 +80,11 @@
     group = local_heads // members
     scale = 1.0 / math.sqrt(HEAD)
 
+    barrier = pltpu.get_barrier_semaphore()
+    for off in range(1, members):
+        pl.semaphore_signal(
+            barrier, inc=1, device_id={"ctx": lax.rem(me + off, members)}, device_id_type=MESH
+        )
     owned = pl.ds(pl.multiple_of(me * (group * HEAD), HEAD), group * HEAD)
     loads = [
         pltpu.make_async_copy(src, dst, load_sem.at[index])
@@ -107,11 +112,6 @@
         return carry
 
     start_stage(0, 0)
-    barrier = pltpu.get_barrier_semaphore()
-    for off in range(1, members):
-        pl.semaphore_signal(
-            barrier, inc=1, device_id={"ctx": lax.rem(me + off, members)}, device_id_type=MESH
-        )
     lax.fori_loop(1, group, start_stage, 0)
     for load in loads[2:]:
         load.start()
@@ -205,7 +205,10 @@
         def _():
             send_inputs(head + AHEAD, 0)
 
-        delta_ref[...] = inbox[head, 0].astype(jnp.float32)
+        for seg in range(SEGS):
+            delta_ref[pl.ds(seg * (steps + 1), steps), :] = inbox[
+                head, 0, pl.ds(seg * steps, steps), :
+            ].astype(jnp.float32)
 
         entering = segment_ends(delta_ref, par_ref, poles, steps, True)
         lams = [row_of(par_ref, 0, pole) for pole in range(poles)]
@@ -214,15 +217,18 @@
         def backward_body(index, states):
             for sub in range(2):
                 step = steps - 1 - (index * 2 + sub)
-                x = delta_ref[pl.ds(step, SEGS, stride=steps), :]
+                x = delta_ref[pl.ds(step, SEGS, stride=steps + 1), :]
                 states = tuple(lam * state + x for lam, state in zip(lams, states))
-                y_ref[pl.ds(step, SEGS, stride=steps), :] = skip * x + tree_sum(
+                y_ref[pl.ds(step, SEGS, stride=steps + 1), :] = skip * x + tree_sum(
                     mix * state for mix, state in zip(mixes, states)
                 )
             return states
 
         lax.fori_loop(0, steps // 2, backward_body, tuple(entering))
-        da_ref[...] = y_ref[...].astype(jnp.bfloat16)
+        for seg in range(SEGS):
+            da_ref[pl.ds(seg * steps, steps), :] = y_ref[
+                pl.ds(seg * (steps + 1), steps), :
+            ].astype(jnp.bfloat16)
 
         key_head = inbox[head, 2]
         value_head = inbox[head, 3]
@@ -237,7 +243,12 @@
             probability = raised * (1.0 / jnp.sum(raised, axis=1, keepdims=True))
             rounded = probability.astype(jnp.bfloat16)
             attended = jnp.dot(rounded, value_head, preferred_element_type=jnp.float32)
-            att_ref[span, :] = attended.astype(jnp.bfloat16).astype(jnp.float32)
+            attended = attended.astype(jnp.bfloat16).astype(jnp.float32)
+            for part in range(rows // steps):
+                seg = block * (rows // steps) + part
+                att_ref[pl.ds(seg * (steps + 1), steps), :] = attended[
+                    part * steps : (part + 1) * steps
+                ]
             weight_adjoint = lax.dot_general(
                 adjoint, value_head, (((1,), (1,)), ((), ())), preferred_element_type=jnp.float32
             )
@@ -273,7 +284,7 @@
                 states, sums = item
                 for sub in range(2):
                     step = index * 2 + sub
-                    here = pl.ds(step, SEGS, stride=steps)
+                    here = pl.ds(step, SEGS, stride=steps + 1)
                     x = att_ref[here, :]
                     delta = delta_ref[here, :]
                     states = tuple(lam * state + x for lam, state in zip(lams, states))
@@ -292,7 +303,10 @@
                     jnp.sum(total, axis=0, keepdims=True) * par_ref[2, pl.ds(pole, 1), :]
                 )
         res_box[head] = par_ref[7].astype(jnp.bfloat16)
-        outbox[head, 3] = y_ref[...].astype(jnp.bfloat16)
+        for seg in range(SEGS):
+            outbox[head, 3, pl.ds(seg * steps, steps), :] = y_ref[
+                pl.ds(seg * (steps + 1), steps), :
+            ].astype(jnp.bfloat16)
         for off in far_first:
             mix_copy(head, off, me).start()
             res_copy(head, off, me).start()
@@ -312,6 +326,10 @@
     def finish(head, carry):
         for off in range(1, members):
             grad_copy(head, off, source(off)).wait_recv()
+        for owner in range(members):
+            for kind in range(3):
+                out_copy(head, owner, kind).start()
+        for off in range(1, members):
             mix_copy(head, off, source(off)).wait_recv()
             res_copy(head, off, source(off)).wait_recv()
         for owner in range(members):
@@ -320,7 +338,7 @@
                 * landed[head, owner, 3].astype(jnp.float32)
             ).astype(jnp.bfloat16)
             res_wide[head, owner] = res_landed[head, owner].astype(jnp.float32)
-            for kind in range(5):
+            for kind in range(3, 5):
                 out_copy(head, owner, kind).start()
         return carry
 
@@ -343,16 +361,13 @@
     sources, targets, held, in_sem, out_sem = refs[:5], refs[5:10], refs[10:15], refs[15], refs[16]
     loads, stores = [], []
     for src, dst, middle in zip(sources, targets, held):
-        width = src.shape[1] // 2
-        for half in range(2):
-            part = pl.ds(half * width, width)
+        pieces = 4 if src.shape[0] % 64 == 0 else 1
+        height = src.shape[0] // pieces
+        for piece in range(pieces):
+            part = pl.ds(piece * height, height)
             index = len(loads)
-            loads.append(
-                pltpu.make_async_copy(src.at[:, part], middle.at[:, part], in_sem.at[index])
-            )
-            stores.append(
-                pltpu.make_async_copy(middle.at[:, part], dst.at[:, part], out_sem.at[index])
-            )
+            loads.append(pltpu.make_async_copy(src.at[part], middle.at[part], in_sem.at[index]))
+            stores.append(pltpu.make_async_copy(middle.at[part], dst.at[part], out_sem.at[index]))
     for load in loads:
         load.start()
     for load, store in zip(loads, stores):
@@ -392,9 +407,9 @@
             pltpu.VMEM((poles, group * HEAD), jnp.float32),
             pltpu.VMEM((1, group * HEAD), jnp.float32),
             pltpu.VMEM((8, poles, HEAD), jnp.float32),
-            pltpu.VMEM((tokens, HEAD), jnp.float32),
-            pltpu.VMEM((tokens, HEAD), jnp.float32),
-            pltpu.VMEM((tokens, HEAD), jnp.float32),
+            pltpu.VMEM((tokens + SEGS, HEAD), jnp.float32),
+            pltpu.VMEM((tokens + SEGS, HEAD), jnp.float32),
+            pltpu.VMEM((tokens + SEGS, HEAD), jnp.float32),
             pltpu.VMEM((tokens, HEAD), jnp.bfloat16),
             pltpu.VMEM((tokens, HEAD), jnp.float32),
             pltpu.VMEM((tokens, HEAD), jnp.float32),
@@ -413,7 +428,7 @@
         in_specs=[hbm] * 5,
         out_specs=(hbm,) * 5,
         scratch_shapes=[pltpu.VMEM(shape.shape, shape.dtype) for shape in shapes]
-        + [pltpu.SemaphoreType.DMA((10,))] * 2,
+        + [pltpu.SemaphoreType.DMA((20,))] * 2,
         compiler_params=pltpu.CompilerParams(vmem_limit_bytes=60 * 1024 * 1024),
     )(*results)
 

time: 104 us -> 104 us (level)
  no operation moved by 1% of the time
where the time goes in v3:
time: 104 us; the launch traced here: 103 us
  Pallas kernels  103 us (99%)
    pallas_call x1, Pallas kernels, fast_local(): pl.pallas_call(functools.partial(fast_kernel, members, local_heads), out_...  100 us
    pallas_call x1, Pallas kernels, fast_local(): pl.pallas_call(write_kernel, out_shape=shapes, in_specs=[hbm] * 5, out_sp...  2.69 us

profile of v3, /device:TPU:0, one launch (start us, length us, event | category | flops | bytes accessed | tf_op | source)
XLA Modules:
  0.0 103.5 jit_solution(13007282302329071665)
XLA Ops:
  0.6 100.2 %shard_map.119 = (bf16[128,2048]{1,0:T(8,128)(2,1)}, bf16[128,2048]{1,0:T(8,128)(2,1)}, bf16[128,2048]{1,0:T(8,128)(2,1)}, bf16[128,2048]{1,0:T(8,128)(2,1)}, f32[16,2048]{1,0:T(8,128)}) custom-call(bf16[128,2048]{1,0:T(8,128)(2,1)} %q_ref.1, bf16[128,2048]{1,0:T(8,128)(2,1)} %k_ref.1, bf16[128,2048]{1,0:T(8,128)(2,1)} %v_ref.1, bf16[128,2048]{1,0:T(8,128)(2,1)} %gate_ref.1, ...), custom_call_target="tpu_custom_call" | custom-call | tf_op jit(solution)/shard_map/pallas_call | solution.py:391
  100.8 2.7 %shard_map.120 = (bf16[128,2048]{1,0:T(8,128)(2,1)}, bf16[128,2048]{1,0:T(8,128)(2,1)}, bf16[128,2048]{1,0:T(8,128)(2,1)}, bf16[128,2048]{1,0:T(8,128)(2,1)}, f32[16,2048]{1,0:T(8,128)}) custom-call(bf16[128,2048]{1,0:T(8,128)(2,1)} %get-tuple-element.10.refs_0_, bf16[128,2048]{1,0:T(8,128)(2,1)} %get-tuple-element.11.refs_1_, ...), custom_call_target="tpu_custom_call" | custom-call | tf_op jit(solution)/shard_map/pallas_call | solution.py:425

commit v4 on v3

--- a/solution.py
+++ b/solution.py
@@ -166,8 +166,12 @@
             res_send.at[head, off - 1], res_recv.at[head, off - 1], dest(off),
         )
 
-    odd = lax.rem(me, 2)
-    far_first = (2, 3 - 2 * odd, 1 + 2 * odd) if members == 4 else tuple(range(1, members))
+    order = tuple(range(1, members))
+    if members == 4:
+        odd = lax.rem(me, 2)
+        turn = lax.rem(lax.axis_index("dp"), 2)
+        near, far = 1 + 2 * odd, 3 - 2 * odd
+        order = (2 + turn * (near - 2), far + turn * (2 - far), near + turn * (far - near))
 
     def send_inputs(head, carry):
         for owner in range(members):
@@ -177,7 +181,7 @@
             ).astype(jnp.bfloat16)
             for kind in range(3):
                 stage_copy(head, owner, kind).wait()
-        for off in far_first:
+        for off in order:
             in_copy(head, off).start()
         return carry
 
@@ -271,7 +275,7 @@
                 dv_acc[...] += value_part
         outbox[head, 1] = dk_acc[...].astype(jnp.bfloat16)
         outbox[head, 2] = dv_acc[...].astype(jnp.bfloat16)
-        for off in far_first:
+        for off in order:
             grad_copy(head, off, me).start()
 
         entering_forward = segment_ends(att_ref, par_ref, poles, steps, False)
@@ -307,7 +311,7 @@
             outbox[head, 3, pl.ds(seg * steps, steps), :] = y_ref[
                 pl.ds(seg * (steps + 1), steps), :
             ].astype(jnp.bfloat16)
-        for off in far_first:
+        for off in order:
             mix_copy(head, off, me).start()
             res_copy(head, off, me).start()
         landed[head, me] = outbox[head, :, rows_of(me), :]
@@ -361,7 +365,7 @@
     sources, targets, held, in_sem, out_sem = refs[:5], refs[5:10], refs[10:15], refs[15], refs[16]
     loads, stores = [], []
     for src, dst, middle in zip(sources, targets, held):
-        pieces = 4 if src.shape[0] % 64 == 0 else 1
+        pieces = 1
         height = src.shape[0] // pieces
         for piece in range(pieces):
             part = pl.ds(piece * height, height)

time: 104 us -> 104 us (level)
  no operation moved by 1% of the time
where the time goes in v4:
time: 104 us
  Pallas kernels  103 us (99%)
    pallas_call x1, Pallas kernels, fast_local(): pl.pallas_call(functools.partial(fast_kernel, members, local_heads), out_...  100 us
    pallas_call x1, Pallas kernels, fast_local(): pl.pallas_call(write_kernel, out_shape=shapes, in_specs=[hbm] * 5, out_sp...  2.74 us

profile of v4, /device:TPU:0, one launch (start us, length us, event | category | flops | bytes accessed | tf_op | source)
XLA Modules:
  0.0 103.5 jit_solution(2317065146733256064)
XLA Ops:
  0.6 100.1 %shard_map.119 = (bf16[128,2048]{1,0:T(8,128)(2,1)}, bf16[128,2048]{1,0:T(8,128)(2,1)}, bf16[128,2048]{1,0:T(8,128)(2,1)}, bf16[128,2048]{1,0:T(8,128)(2,1)}, f32[16,2048]{1,0:T(8,128)}) custom-call(bf16[128,2048]{1,0:T(8,128)(2,1)} %q_ref.1, bf16[128,2048]{1,0:T(8,128)(2,1)} %k_ref.1, bf16[128,2048]{1,0:T(8,128)(2,1)} %v_ref.1, bf16[128,2048]{1,0:T(8,128)(2,1)} %gate_ref.1, ...), custom_call_target="tpu_custom_call" | custom-call | tf_op jit(solution)/shard_map/pallas_call | solution.py:395
  100.8 2.7 %shard_map.120 = (bf16[128,2048]{1,0:T(8,128)(2,1)}, bf16[128,2048]{1,0:T(8,128)(2,1)}, bf16[128,2048]{1,0:T(8,128)(2,1)}, bf16[128,2048]{1,0:T(8,128)(2,1)}, f32[16,2048]{1,0:T(8,128)}) custom-call(bf16[128,2048]{1,0:T(8,128)(2,1)} %get-tuple-element.10.refs_0_, bf16[128,2048]{1,0:T(8,128)(2,1)} %get-tuple-element.11.refs_1_, ...), custom_call_target="tpu_custom_call" | custom-call | tf_op jit(solution)/shard_map/pallas_call | solution.py:429

commit v5 on v3

--- a/solution.py
+++ b/solution.py
@@ -106,17 +106,10 @@
         )
 
     def start_stage(head, carry):
-        for owner in range(members):
-            for kind in range(3):
-                stage_copy(head, owner, kind).start()
+        for kind in range(3):
+            stage_copy(head, me, kind).start()
         return carry
 
-    start_stage(0, 0)
-    lax.fori_loop(1, group, start_stage, 0)
-    for load in loads[2:]:
-        load.start()
-    for load in loads[:2]:
-        load.wait()
     pl.semaphore_wait(barrier, members - 1)
 
     def rows_of(owner):
@@ -134,16 +127,14 @@
             device_id={"ctx": target}, device_id_type=MESH,
         )
 
-    def in_copy(head, off):
+    def in_copy(head, off, kind, owner):
+        if kind == 0:
+            src = stage.at[head, dest(off), 0]
+        else:
+            src = (q_ref, k_ref, v_ref)[kind - 1].at[:, lanes(dest(off), head)]
         return remote(
-            stage.at[head, dest(off)], inbox.at[head, :, rows_of(me), :],
-            in_send.at[head, off - 1], in_recv.at[head, off - 1], dest(off),
-        )
-
-    def in_arrival(head, off):
-        return remote(
-            stage.at[head, dest(off)], inbox.at[head, :, rows_of(source(off)), :],
-            in_send.at[head, off - 1], in_recv.at[head, off - 1], dest(off),
+            src, inbox.at[head, kind, rows_of(owner), :],
+            in_send.at[head, off - 1, kind], in_recv.at[head, off - 1, kind], dest(off),
         )
 
     def grad_copy(head, off, owner):
@@ -169,19 +160,32 @@
     odd = lax.rem(me, 2)
     far_first = (2, 3 - 2 * odd, 1 + 2 * odd) if members == 4 else tuple(range(1, members))
 
-    def send_inputs(head, carry):
+    def send_rows(head, carry):
+        for kind in range(1, 4):
+            for off in far_first:
+                in_copy(head, off, kind, me).start()
+        return carry
+
+    def send_delta(head, carry):
         for owner in range(members):
             here = lanes(owner, head)
             stage[head, owner, 0] = (
                 cot_v[:, here].astype(jnp.float32) * gate_v[:, here].astype(jnp.float32)
             ).astype(jnp.bfloat16)
-            for kind in range(3):
-                stage_copy(head, owner, kind).wait()
         for off in far_first:
-            in_copy(head, off).start()
+            in_copy(head, off, 0, me).start()
         return carry
 
-    lax.fori_loop(0, min(AHEAD, group), send_inputs, 0)
+    send_rows(0, 0)
+    lax.fori_loop(0, group, start_stage, 0)
+    for load in loads[2:]:
+        load.start()
+    for load in loads[:2]:
+        load.wait()
+    send_delta(0, 0)
+    for head in range(1, min(AHEAD, group)):
+        send_rows(head, 0)
+        send_delta(head, 0)
     for load in loads[2:]:
         load.wait()
 
@@ -197,13 +201,17 @@
         par_ref[5] = jnp.exp(-damping * (4 * steps))
         par_ref[6] = 1.0 / (1.0 - jnp.exp(-damping * tokens))
         skip = jnp.broadcast_to(skip_v[:, mine], (SEGS, HEAD))
+        for kind in range(3):
+            stage_copy(head, me, kind).wait()
         inbox[head, :, rows_of(me), :] = stage[head, me]
         for off in range(1, members):
-            in_arrival(head, off).wait_recv()
+            for kind in range(4):
+                in_copy(head, off, kind, source(off)).wait_recv()
 
         @pl.when(head + AHEAD < group)
         def _():
-            send_inputs(head + AHEAD, 0)
+            send_rows(head + AHEAD, 0)
+            send_delta(head + AHEAD, 0)
 
         for seg in range(SEGS):
             delta_ref[pl.ds(seg * (steps + 1), steps), :] = inbox[
@@ -345,7 +353,8 @@
     lax.fori_loop(0, group, finish, 0)
     def sent(head, carry):
         for off in range(1, members):
-            in_copy(head, off).wait_send()
+            for kind in range(4):
+                in_copy(head, off, kind, me).wait_send()
             grad_copy(head, off, me).wait_send()
             mix_copy(head, off, me).wait_send()
             res_copy(head, off, me).wait_send()
@@ -361,13 +370,16 @@
     sources, targets, held, in_sem, out_sem = refs[:5], refs[5:10], refs[10:15], refs[15], refs[16]
     loads, stores = [], []
     for src, dst, middle in zip(sources, targets, held):
-        pieces = 4 if src.shape[0] % 64 == 0 else 1
-        height = src.shape[0] // pieces
-        for piece in range(pieces):
-            part = pl.ds(piece * height, height)
+        width = src.shape[1] // 2
+        for half in range(2):
+            part = pl.ds(half * width, width)
             index = len(loads)
-            loads.append(pltpu.make_async_copy(src.at[part], middle.at[part], in_sem.at[index]))
-            stores.append(pltpu.make_async_copy(middle.at[part], dst.at[part], out_sem.at[index]))
+            loads.append(
+                pltpu.make_async_copy(src.at[:, part], middle.at[:, part], in_sem.at[index])
+            )
+            stores.append(
+                pltpu.make_async_copy(middle.at[:, part], dst.at[:, part], out_sem.at[index])
+            )
     for load in loads:
         load.start()
     for load, store in zip(loads, stores):
@@ -413,7 +425,7 @@
             pltpu.VMEM((tokens, HEAD), jnp.bfloat16),
             pltpu.VMEM((tokens, HEAD), jnp.float32),
             pltpu.VMEM((tokens, HEAD), jnp.float32),
-        ] + [sems] * 8 + [
+        ] + [pltpu.SemaphoreType.DMA((group, members - 1, 4))] * 2 + [sems] * 6 + [
             pltpu.SemaphoreType.DMA((5,)), pltpu.SemaphoreType.DMA((group, members, 3)),
             pltpu.SemaphoreType.DMA((group, members, 5)),
         ],
@@ -428,7 +440,7 @@
         in_specs=[hbm] * 5,
         out_specs=(hbm,) * 5,
         scratch_shapes=[pltpu.VMEM(shape.shape, shape.dtype) for shape in shapes]
-        + [pltpu.SemaphoreType.DMA((20,))] * 2,
+        + [pltpu.SemaphoreType.DMA((10,))] * 2,
         compiler_params=pltpu.CompilerParams(vmem_limit_bytes=60 * 1024 * 1024),
     )(*results)
 

time: 104 us -> 104 us (level)
  no operation moved by 1% of the time
where the time goes in v5:
time: 104 us
  Pallas kernels  103 us (99%)
    pallas_call x1, Pallas kernels, fast_local(): pl.pallas_call(functools.partial(fast_kernel, members, local_heads), out_...  101 us
    pallas_call x1, Pallas kernels, fast_local(): pl.pallas_call(write_kernel, out_shape=shapes, in_specs=[hbm] * 5, out_sp...  2.47 us

profile of v5, /device:TPU:0, one launch (start us, length us, event | category | flops | bytes accessed | tf_op | source)
XLA Modules:
  0.0 103.7 jit_solution(15923737735294916156)
XLA Ops:
  0.6 100.6 %shard_map.119 = (bf16[128,2048]{1,0:T(8,128)(2,1)}, bf16[128,2048]{1,0:T(8,128)(2,1)}, bf16[128,2048]{1,0:T(8,128)(2,1)}, bf16[128,2048]{1,0:T(8,128)(2,1)}, f32[16,2048]{1,0:T(8,128)}) custom-call(bf16[128,2048]{1,0:T(8,128)(2,1)} %q_ref.1, bf16[128,2048]{1,0:T(8,128)(2,1)} %k_ref.1, bf16[128,2048]{1,0:T(8,128)(2,1)} %v_ref.1, bf16[128,2048]{1,0:T(8,128)(2,1)} %gate_ref.1, ...), custom_call_target="tpu_custom_call" | custom-call | tf_op jit(solution)/shard_map/pallas_call | solution.py:403
  101.2 2.5 %shard_map.120 = (bf16[128,2048]{1,0:T(8,128)(2,1)}, bf16[128,2048]{1,0:T(8,128)(2,1)}, bf16[128,2048]{1,0:T(8,128)(2,1)}, bf16[128,2048]{1,0:T(8,128)(2,1)}, f32[16,2048]{1,0:T(8,128)}) custom-call(bf16[128,2048]{1,0:T(8,128)(2,1)} %get-tuple-element.10.refs_0_, bf16[128,2048]{1,0:T(8,128)(2,1)} %get-tuple-element.11.refs_1_, ...), custom_call_target="tpu_custom_call" | custom-call | tf_op jit(solution)/shard_map/pallas_call | solution.py:437
